TPU v7x, 512 devices: a whole 4x8x8 slice. The times are simulated.
512 devices in a mesh: ex: 128 (over y, z, core), pp: 4 (over x).
Axes of the slice: x: 4, y: 8, z: 8, core: 2. Of those that a mesh axis runs over, the one named last changes fastest.
Arguments:
- activations: bfloat16 [256, 128, 64, 128], P('ex', 'pp'), may hold values from -2 to 2
- output_grads: bfloat16 [256, 128, 32, 128], P('ex', 'pp'), may hold values from -2 to 2
- lengths: int32 [256], P('ex'), may hold values from 32 to 128
- whitening: bfloat16 [128, 4, 512, 2048], P('ex', 'pp'), may hold values from -0.125 to 0.125
Outputs:
- influence: float32 [128, 128], P('ex')
Inputs may be any that keep to these rules, and one draw needn't show every extreme that they name: Positions from lengths[e] on are padding of example e.
All inputs are finite; a program needn't handle non-finite values.
Results may differ from a plain program's by a relative error of at most 0.0047.
Values may be sent and summed in bfloat16 or wider, within the bound.
A program may use at most 64 MiB of HBM per device.

v0:
```python
import math

import jax
import jax.numpy as jnp
from jax import lax
from jax.sharding import Mesh
from jax.sharding import PartitionSpec as P

ITERS = 3
EX = ("ex_0", "ex_1", "ex_2")


step_rate = 0.5
ridge_shift = 0.5
clip_frac = 0.06


def filled_up(lines, size):
    spare = -len(lines) % size
    return jnp.pad(lines, [(0, spare)] + [(0, 0)] * (lines.ndim - 1))


def copy_for_each(value, axis):
    copies = jnp.broadcast_to(value, (lax.axis_size(axis), *value.shape))
    return lax.all_to_all(copies, axis, split_axis=0, concat_axis=0, tiled=True)


def in_order(tiles, dim):
    tiles = jnp.moveaxis(tiles, 0, dim)
    lengths = tiles.shape
    return tiles.reshape(*lengths[:dim], lengths[dim] * lengths[dim + 1], *lengths[dim + 2 :])


def gather_axes(value, axes, dim):
    far, near = axes
    first = copy_for_each(value, far)
    tiles = jnp.swapaxes(copy_for_each(first, near), 0, 1)
    return in_order(tiles.reshape(-1, *value.shape), dim)


def cut_along(value, dim, size):
    before, after = (value.shape[:dim], value.shape[dim + 1 :])
    return jnp.moveaxis(value.reshape(*before, size, -1, *after), dim, 0)


def summed_on_arrival(value, axis, dim):
    tiles = cut_along(value, dim, lax.axis_size(axis))
    arrived = lax.all_to_all(tiles, axis, split_axis=0, concat_axis=0, tiled=True)
    return arrived.sum(axis=0)


def sum_in_two_steps(value, axes, dim):
    far, near = axes
    own = summed_on_arrival(cut_along(value, dim, lax.axis_size(far)), near, dim + 1)
    return jnp.sum(lax.all_to_all(own, far, 0, 0, tiled=True), axis=0)


def total_of(value, axes):
    padded = filled_up(value, lax.axis_size(axes[0]) * lax.axis_size(axes[1]))
    whole = gather_axes(sum_in_two_steps(padded, axes, 0), axes, 0)
    return lax.slice_in_dim(whole, 0, len(value)).reshape(value.shape)


def packed_total(arrays, axis):
    ends = [0]
    for a in arrays:
        ends.append(ends[-1] + a.size)
    total = total_of(jnp.concatenate([a.ravel() for a in arrays]), axis)
    return tuple((total[b:e].reshape(a.shape) for a, b, e in zip(arrays, ends, ends[1:])))


def refine(scores, kernel, total_fn, clip_level):
    answer = jnp.zeros_like(scores)
    for iteration in range(ITERS):
        residual = (
            scores - jnp.dot(answer, kernel, precision=lax.Precision.HIGHEST) - ridge_shift * answer
        )
        magnitude = jnp.sqrt(total_fn(jnp.sum(residual * residual)) + 1e-06)
        answer = answer + jnp.minimum(step_rate, clip_level / magnitude) * residual
    return answer


def keep_local(value):
    return value


def body(activations, output_grads, lengths, whitening):
    ex_dev, mod_segment, k_in, seq_len = activations.shape
    slab_rows = whitening.shape[2]
    feat_count = whitening.shape[3]
    group_size = feat_count // slab_rows
    n_ex = lax.axis_size(EX)
    n_pp = lax.axis_size("pp")
    examples = ex_dev * n_ex
    queries = examples // 2
    train_count = examples - queries
    token_mask = (lax.broadcasted_iota(jnp.int32, (ex_dev, seq_len), 1) < lengths[:, None]).astype(
        jnp.bfloat16
    )
    masked = output_grads * token_mask[:, None, None, :]
    every_block = jnp.einsum(
        "emkt,emjt->mekj", masked, activations, preferred_element_type=jnp.float32
    )
    every_block = every_block.astype(jnp.bfloat16).reshape(mod_segment, 1, ex_dev, feat_count)
    sending = jnp.broadcast_to(every_block, (mod_segment, group_size, ex_dev, feat_count)).reshape(
        n_ex, ex_dev, feat_count
    )
    features = lax.all_to_all(sending, EX, split_axis=0, concat_axis=0, tiled=True).reshape(
        examples, feat_count
    )
    whiten_slab = whitening.reshape(slab_rows, feat_count)
    whitened = lax.dot_general(
        features, whiten_slab, (((1,), (1,)), ((), ())), preferred_element_type=jnp.float32
    ).astype(jnp.bfloat16)
    query_part = whitened[:queries]
    train_part = whitened[queries:]
    cross_part = lax.dot_general(
        query_part, train_part, (((1,), (1,)), ((), ())), preferred_element_type=jnp.float32
    )
    train_gram = lax.dot_general(
        train_part, train_part, (((1,), (1,)), ((), ())), preferred_element_type=jnp.float32
    )
    count_all = mod_segment * n_pp * feat_count
    root_scale = 1.0 / math.sqrt(count_all)
    gram_scale = 1.0 / count_all
    clip_level = clip_frac * math.sqrt(queries * train_count)
    query_share = queries // n_ex
    cross_sum, gram_sum = packed_total((cross_part, train_gram), (("ex_0", "ex_1"), ("ex_2", "pp")))
    answer = refine(cross_sum * root_scale, gram_sum * gram_scale, keep_local, clip_level)
    return lax.dynamic_slice_in_dim(answer, lax.axis_index(EX) * query_share, query_share, 0)


def solution(mesh):
    finer = Mesh(mesh.devices.reshape(8, 8, 2, mesh.shape["pp"]), ("ex_0", "ex_1", "ex_2", "pp"))
    placed = (P(EX, "pp", None, None), P(EX, "pp", None, None), P(EX), P(EX, "pp", None, None))
    return jax.shard_map(body, mesh=finer, in_specs=placed, out_specs=P(EX, None), check_vma=False)
```

profile of v0, /device:TPU:1, one launch (start us, length us, event | category | flops | bytes accessed | tf_op | source)
XLA Modules:
  0.0 118.1 jit_solution(4898977391090082254)
XLA Ops:
  0.0 0.0 copy-start
  0.0 0.9 compare_convert_fusion
  0.9 2.0 %convolution_convert_fusion = bf16[32,2,32,64]{3,2,1,0:T(8,128)(2,1)S(1)} fusion(bf16[2,32,64,128]{3,2,1,0:T(8,128)(2,1)} %param.4, bf16[2,32,32,128]{3,2,1,0:T(8,128)(2,1)} %param.5, bf16[2,128]{1,0:T(2,128)(2,1)S(1)} %compare_convert_fusion), kind=kOutput, calls=%fused_computation.2 | convolution fusion | flops 33947648 | bytes 1835520 | tf_op jit(solution)/shard_map/emkt,emjt->mekj/dot_general | solution.py:101
  2.9 0.4 broadcast_in_dim.16
  3.3 0.6 broadcast_in_dim.17
  4.0 48.7 %all_to_all.33 = bf16[128,2,2048]{2,1,0:T(2,128)(2,1)S(1)} all-to-all(bf16[128,2,2048]{2,1,0:T(2,128)(2,1)S(1)} %bitcast.19), channel_id=1, replica_groups=mesh['ex_0'=8,'ex_1'=8,'ex_2'=2,'pp'=4] {'ex_0','ex_1','ex_2'}, dimensions={0} | all-to-all | bytes 2097152 | tf_op jit(solution)/shard_map/all_to_all | solution.py:108
  52.6 1.2 %reshape.56 = bf16[256,2048]{1,0:T(8,128)(2,1)} reshape(bf16[128,2,2048]{2,1,0:T(2,128)(2,1)S(1)} %all_to_all.33) | data formatting | bytes 2097152 | tf_op jit(solution)/shard_map/reshape | solution.py:108
  53.8 0.0 copy-done
  53.8 2.0 %fusion.2 = bf16[256,512]{1,0:T(8,128)(2,1)S(1)} fusion(bf16[256,2048]{1,0:T(8,128)(2,1)} %reshape.56, bf16[1,1,512,2048]{3,2,1,0:T(8,128)(2,1)S(1)} %copy-done), kind=kOutput, calls=%fused_computation.3 | convolution fusion | flops 537001984 | bytes 3407872 | tf_op jit(solution)/shard_map/dot_general | solution.py:112
  55.8 0.2 fusion.9
  56.0 0.2 fusion.11
  56.2 0.1 concatenate.8
  56.3 0.1 concatenate.9
  56.5 0.2 reshape.58
  56.7 10.6 %all_to_all.34 = f32[8,1,4096]{2,1,0:T(1,128)S(1)} all-to-all(f32[8,1,4096]{2,1,0:T(1,128)S(1)} %reshape.58), channel_id=1, replica_groups=mesh['ex_0'=8,'ex_1'=8,'ex_2'=2,'pp'=4] {'ex_2','pp'}, dimensions={0} | all-to-all | bytes 262144 | tf_op jit(solution)/shard_map/all_to_all | solution.py:48
  67.2 0.5 broadcast.34
  67.8 1.0 reduce.9
  68.7 0.1 reshape.59
  68.9 15.6 %all_to_all.35 = f32[64,1,64]{2,1,0:T(1,128)S(1)} all-to-all(f32[64,1,64]{2,1,0:T(1,128)S(1)} %bitcast.23), channel_id=1, replica_groups=mesh['ex_0'=8,'ex_1'=8,'ex_2'=2,'pp'=4] {'ex_0','ex_1'}, dimensions={0} | all-to-all | bytes 32768 | tf_op jit(solution)/shard_map/all_to_all | solution.py:55
  84.5 0.1 reduce_sum.46
  84.6 14.6 %all_to_all.36 = f32[64,1,64]{2,1,0:T(1,128)S(1)} all-to-all(f32[64,1,64]{2,1,0:T(1,128)S(1)} %broadcast_in_dim.18), channel_id=1, replica_groups=mesh['ex_0'=8,'ex_1'=8,'ex_2'=2,'pp'=4] {'ex_0','ex_1'}, dimensions={0} | all-to-all | bytes 32768 | tf_op jit(solution)/shard_map/all_to_all | solution.py:25
  99.2 0.8 reshape.60
  100.1 6.2 %all-to-all-start.4 = ((f32[8,1,4096]{2,1,0:T(1,128)}), f32[8,1,4096]{2,1,0:T(1,128)S(1)}, u32[]{:S(2)}, u32[]{:S(2)}) async-start(f32[8,1,4096]{2,1,0:T(1,128)} %reshape.60), calls=%async_computation.4 | async-start | bytes 262144 | tf_op jit(solution)/shard_map/all_to_all | solution.py:25
  106.3 5.2 %all-to-all-done.4 = f32[8,1,4096]{2,1,0:T(1,128)S(1)} async-done(((f32[8,1,4096]{2,1,0:T(1,128)}), f32[8,1,4096]{2,1,0:T(1,128)S(1)}, u32[]{:S(2)}, u32[]{:S(2)}) %all-to-all-start.4) | async-done | bytes 131104 | tf_op jit(solution)/shard_map/all_to_all | solution.py:25
  111.5 1.0 reduce.10
  112.4 0.1 reshape.61
  112.6 0.1 copy.16
  112.6 0.1 mul.82
  112.8 0.1 dot_general.33
  112.9 0.6 multiply_reduce_fusion
  114.2 0.1 copy.17
  114.3 0.1 mul.85
  114.4 0.1 copy.18
  114.5 0.1 mul.89
  114.6 0.8 multiply_reduce_fusion.2
  116.1 0.8 multiply_reduce_fusion.1
  117.6 0.5 dynamic-slice_add_fusion
  (11 shorter events, 0.2 us)
Async XLA Ops:
  0.0 53.8 %copy-start = (bf16[1,1,512,2048]{3,2,1,0:T(8,128)(2,1)S(1)}, bf16[1,1,512,2048]{3,2,1,0:T(8,128)(2,1)}, u32[]{:S(2)}) copy-start(bf16[1,1,512,2048]{3,2,1,0:T(8,128)(2,1)} %param.7) | copy-start | bytes 6291460
  100.1 11.4 %all-to-all-start.4 = ((f32[8,1,4096]{2,1,0:T(1,128)}), f32[8,1,4096]{2,1,0:T(1,128)S(1)}, u32[]{:S(2)}, u32[]{:S(2)}) async-start(f32[8,1,4096]{2,1,0:T(1,128)} %reshape.60), calls=%async_computation.4 | async-start | bytes 262144 | tf_op jit(solution)/shard_map/all_to_all | solution.py:25
where the time goes:
time: 119 us; the launch traced here: 118 us
  blocking collectives  89.5 us (75%)
  starting transfers between devices  6.25 us (5%)
  matrix products  5.98 us (5%)
  waiting for transfers between devices  5.16 us (4%)
  local copies, waits for them, and re-layouts  4.81 us (4%)
  other arithmetic  4.16 us (3%)
  between operations  2.27 us (2%)
    all_to_all x1, blocking collectives, body(): lax.all_to_all(sending, EX, split_axis=0, concat_axis=0, tiled=True)  48.7 us
    all_to_all x1, blocking collectives, sum_in_two_steps(): return jnp.sum(lax.all_to_all(own, far, 0, 0, tiled=True), axis=0)  15.6 us
    all_to_all x1, blocking collectives, copy_for_each(): return lax.all_to_all(copies, axis, split_axis=0, concat_axis=0, tiled=True)  14.6 us
    all_to_all x1, blocking collectives, summed_on_arrival(): lax.all_to_all(tiles, axis, split_axis=0, concat_axis=0, tiled=True)  10.6 us
    all_to_all x1, starting transfers between devices, copy_for_each(): return lax.all_to_all(copies, axis, split_axis=0, concat_axis=0, tiled=True)  6.25 us
    all_to_all x1, waiting for transfers between devices, copy_for_each(): return lax.all_to_all(copies, axis, split_axis=0, concat_axis=0, tiled=True)  5.16 us
  transfers between devices with their start and end apart: 1, of which 1 were waited for; matrix products, arithmetic and copies ran while one was open for 0% of the time, Pallas kernels for 0%

commit v1 on v0

v1 whole, which is shorter than its diff:
```python
import functools
import math

import jax
import jax.numpy as jnp
from jax import lax
from jax.experimental import pallas as pl
from jax.experimental.pallas import tpu as pltpu
from jax.sharding import PartitionSpec as P

MESH = pl.DeviceIdType.MESH
BF = jnp.bfloat16
F32 = jnp.float32
NY, NZ, NC, NX = 8, 8, 2, 4
NT = (((1,), (1,)), ((), ()))

step_rate = 0.5
ridge_shift = 0.5
clip_frac = 0.06


def total(value):
    return jnp.sum(jnp.sum(value, axis=1, keepdims=True), axis=0, keepdims=True)


def kernel(
    len_ref, act_hbm, grad_hbm, w_hbm, out_ref,
    act, grad, w_in, w, gbuf, near_buf, feat, white, part, rs_z, rs_y, rs_x, mine, full, answer,
    in_sem, w_sem, p1_send, p1_recv, p2_send, p2_recv, rs_send, rs_recv,
):
    ex = lax.axis_index("ex")
    x = lax.axis_index("pp")
    y = ex // (NZ * NC)
    z = (ex // NC) % NZ
    c = ex % NC
    half = y // 4
    odd = z % 2
    mate_z = z + 1 - 2 * odd

    def at(y_, z_, c_, x_=None):
        return ((y_ * NZ + z_) * NC + c_, x if x_ is None else x_)

    def row_of(i):
        return (half + i // 4) % 2 * 4 + (y + i) % 4

    def load(i):
        rows = pl.ds(row_of(i) * 4, 4)
        return (
            pltpu.make_async_copy(act_hbm.at[:, rows], act.at[:, rows], in_sem.at[0, i]),
            pltpu.make_async_copy(grad_hbm.at[:, rows], grad.at[:, rows], in_sem.at[1, i]),
        )

    for i in range(NY):
        for copy in load(i):
            copy.start()
    w_copy = pltpu.make_async_copy(w_hbm.at[0, 0], w_in, w_sem)
    w_copy.start()

    barrier = pltpu.get_barrier_semaphore()
    toward = 2 * odd - 1

    def greet(i, _):
        y_, d = i // 4, i % 4

        @pl.when(jnp.logical_not(jnp.logical_and(y_ == y, d == 0)))
        def _():
            z_ = (z + toward * d + NZ) % NZ
            pl.semaphore_signal(barrier, inc=1, device_id=at(y_, z_, c), device_id_type=MESH)

        return 0

    lax.fori_loop(0, 32, greet, 0)
    for i in range(1, 16):
        j = (z * NC + c + i) % 16
        pl.semaphore_signal(barrier, inc=1, device_id=at(y, j // NC, j % NC), device_id_type=MESH)
    for i in range(1, NX):
        pl.semaphore_signal(barrier, inc=1, device_id=at(y, z, c, (x + i) % NX), device_id_type=MESH)

    lane_low = lax.broadcasted_iota(jnp.int32, (16, 128), 1) < 64
    spots = lax.broadcasted_iota(jnp.int32, (1, 128), 1)
    masks = [(spots < len_ref[e]).astype(F32).astype(BF) for e in range(2)]

    s_own = ((z + 1) // 2) % 4
    zl = (z + 1) % 2
    slot = (y % 4) * 2 + zl

    def target(p):
        d = (2 * p - z + NZ) % NZ
        chip = jnp.where(d < 4, 2 * p, 2 * p + 1)
        far = jnp.where(d < 4, d // 2, (7 - d) // 2)
        return chip, far

    def gradients(i):
        y_ = row_of(i)
        for copy in load(i):
            copy.wait()
        for k in range(4):
            m = y_ * 4 + k
            for e in range(2):
                a = act[e, m]
                g = grad[e, m] * masks[e]
                twice = jnp.concatenate([a, a], axis=0)
                both = lax.dot_general(g, twice, NT, preferred_element_type=F32)
                gbuf[m, e] = jnp.where(lane_low, both[:16], both[16:]).astype(BF)

    def send(i, _):
        y_ = row_of(i)
        for p in range(4):
            m = y_ * 4 + p
            chip, far = target(p)
            here = jnp.logical_and(y_ == y, chip == z)

            @pl.when(here)
            def _():
                pltpu.make_async_copy(
                    gbuf.at[m], near_buf.at[half, far, slot], p1_recv.at[half, far]
                ).start()

            @pl.when(jnp.logical_not(here))
            def _():
                pltpu.make_async_remote_copy(
                    src_ref=gbuf.at[m],
                    dst_ref=near_buf.at[half, far, slot],
                    send_sem=p1_send,
                    recv_sem=p1_recv.at[half, far],
                    device_id=at(y_, chip, c),
                    device_id_type=MESH,
                ).start()

    gradients(0)
    pl.semaphore_wait(barrier, 31 + 15 + 3)
    send(0, 0)

    def produce(i, _):
        gradients(i)
        send(i, 0)
        return 0

    lax.fori_loop(1, NY, produce, 0)

    w_copy.wait()

    def reorder(r, _):
        rows = pl.ds(r * 32, 32)
        low = lax.broadcasted_iota(jnp.int32, (32, 128), 1) < 64
        for a in range(8):
            t = w_in[rows, a * 128:(a + 1) * 128]
            u = w_in[rows, (8 + a) * 128:(9 + a) * 128]
            t_turned = jnp.concatenate([t[:, 64:], t[:, :64]], axis=1)
            u_turned = jnp.concatenate([u[:, 64:], u[:, :64]], axis=1)
            w[rows, 2 * a * 128:(2 * a + 1) * 128] = jnp.where(low, t, u_turned)
            w[rows, (2 * a + 1) * 128:(2 * a + 2) * 128] = jnp.where(low, t_turned, u)
        return 0

    lax.fori_loop(0, 16, reorder, 0)

    to = lax.broadcasted_iota(jnp.int32, (256, 256), 0)
    frm = lax.broadcasted_iota(jnp.int32, (256, 256), 1)
    shuffle = (frm == (to % 16) * 16 + to // 16).astype(F32).astype(BF)

    def block_rows(q, z_, c_):
        h = (half + q // 2) % 2
        p = z_ // 2
        s = jnp.where(z_ % 2 == 0, p - q % 2 + 4, p + 1 + q % 2) % 4
        return pl.ds(pl.multiple_of(h * 128 + s * 32 + c_ * 16, 16), 16)

    def pair_copy(kind, q):
        rows = block_rows(q, mate_z if kind == 2 else z, c)
        return pltpu.make_async_remote_copy(
            src_ref=feat.at[rows],
            dst_ref=feat.at[rows],
            send_sem=p2_send.at[kind, q],
            recv_sem=p2_recv.at[kind, q],
            device_id=at(y, mate_z, c) if kind == 0 else at(y, z, 1 - c),
            device_id_type=MESH,
        )

    def arrived(kind, q):
        rows = block_rows(q, z if kind == 1 else mate_z, c if kind == 0 else 1 - c)
        pltpu.make_async_copy(feat.at[rows], feat.at[rows], p2_recv.at[kind, q]).wait()

    def whiten(h):
        rows = pl.ds(pl.multiple_of(h * 128, 128), 128)
        white[rows] = lax.dot_general(feat[rows], w[...], NT, preferred_element_type=F32).astype(BF)

    for q in range(4):
        h = (half + q // 2) % 2
        block = near_buf.at[h, q % 2]
        pltpu.make_async_copy(block, block, p1_recv.at[h, q % 2]).wait()
        tiles = near_buf[h, q % 2].reshape(256, 128)
        turned = jnp.dot(shuffle, tiles, preferred_element_type=F32).astype(BF)
        rows = block_rows(q, z, c)
        for kk in range(16):
            feat[rows, kk * 128:(kk + 1) * 128] = turned[kk * 16:(kk + 1) * 16]
        pair_copy(0, q).start()
        pair_copy(1, q).start()
        if q > 0:
            arrived(0, q - 1)
            pair_copy(2, q - 1).start()
    for q in range(2):
        arrived(1, q)
        arrived(2, q)
    whiten(half)
    arrived(0, 3)
    pair_copy(2, 3).start()
    for q in range(2, 4):
        arrived(1, q)
        arrived(2, q)
    whiten((half + 1) % 2)

    part[...] = lax.dot_general(white[...], white[128:], NT, preferred_element_type=F32)

    me16 = z * NC + c
    for i in range(1, 16):
        j = (me16 + i) % 16
        pltpu.make_async_remote_copy(
            src_ref=part.at[pl.ds(pl.multiple_of(j * 16, 16), 16)],
            dst_ref=rs_z.at[15 - i],
            send_sem=rs_send.at[0],
            recv_sem=rs_recv.at[0],
            device_id=at(y, j // NC, j % NC),
            device_id_type=MESH,
        ).start()
    own = part[pl.ds(pl.multiple_of(me16 * 16, 16), 16)]
    pltpu.make_async_copy(rs_z, rs_z, rs_recv.at[0]).wait()
    mine[0] = own + jnp.sum(rs_z[...], axis=0)

    for i in range(1, NY):
        pltpu.make_async_remote_copy(
            src_ref=mine.at[0],
            dst_ref=rs_y.at[y],
            send_sem=rs_send.at[1],
            recv_sem=rs_recv.at[1],
            device_id=at((y + i) % NY, z, c),
            device_id_type=MESH,
        ).start()
    rs_y[y] = mine[0]
    pltpu.make_async_copy(rs_y.at[1:], rs_y.at[1:], rs_recv.at[1]).wait()
    mine[1] = jnp.sum(rs_y[...], axis=0)

    for i in range(1, NX):
        pltpu.make_async_remote_copy(
            src_ref=mine.at[1],
            dst_ref=rs_x.at[x],
            send_sem=rs_send.at[2],
            recv_sem=rs_recv.at[2],
            device_id=at(y, z, c, (x + i) % NX),
            device_id_type=MESH,
        ).start()
    rs_x[x] = mine[1]
    pltpu.make_async_copy(rs_x.at[1:], rs_x.at[1:], rs_recv.at[2]).wait()
    my_rows = pl.ds(pl.multiple_of(me16 * 16, 16), 16)
    full[my_rows] = jnp.sum(rs_x[...], axis=0)

    for i in range(1, 16):
        j = (me16 + i) % 16
        pltpu.make_async_remote_copy(
            src_ref=full.at[my_rows],
            dst_ref=full.at[my_rows],
            send_sem=rs_send.at[3],
            recv_sem=rs_recv.at[3],
            device_id=at(y, j // NC, j % NC),
            device_id_type=MESH,
        ).start()
    pltpu.make_async_copy(full.at[:240], full.at[:240], rs_recv.at[3]).wait()

    count = 32 * NX * 2048
    scores = full[:128] * (1.0 / math.sqrt(count))
    gram = full[128:] * (1.0 / count)
    level = clip_frac * math.sqrt(128 * 128)
    exact = functools.partial(jnp.dot, precision=lax.Precision.HIGHEST, preferred_element_type=F32)

    def pace(residual):
        return jnp.minimum(step_rate, level * lax.rsqrt(total(residual * residual) + 1e-06))

    now = pace(scores) * scores
    for _ in range(2):
        residual = scores - exact(now, gram) - ridge_shift * now
        now = now + pace(residual) * residual
    answer[...] = now

    q_y, q_z, q_c, q_e = ex // 32, (ex // 4) % 8, (ex // 2) % 2, ex % 2
    row = ((q_z + 1) // 2) % 4 * 32 + q_c * 16 + q_y * 4 + (q_z + 1) % 2 * 2 + q_e
    line = jnp.broadcast_to(answer[pl.ds(row, 1)], (8, 128))
    t = lax.broadcasted_iota(jnp.int32, (128, 128), 1)
    t_z = (t // 4) % 8
    spot = ((t_z + 1) // 2) % 4 * 32 + (t // 2) % 2 * 16 + t // 32 * 4 + (t_z + 1) % 2 * 2 + t % 2
    pick = (lax.broadcasted_iota(jnp.int32, (128, 128), 0) == spot).astype(F32)
    out_ref[...] = exact(line, pick)[:1]

    pltpu.make_async_copy(gbuf.at[:31], gbuf.at[:31], p1_send).wait()
    for kind in range(3):
        for q in range(4):
            pair_copy(kind, q).wait_send()
    pltpu.make_async_copy(rs_z, rs_z, rs_send.at[0]).wait()
    pltpu.make_async_copy(rs_y.at[1:], rs_y.at[1:], rs_send.at[1]).wait()
    pltpu.make_async_copy(rs_x.at[1:], rs_x.at[1:], rs_send.at[2]).wait()
    pltpu.make_async_copy(full.at[:240], full.at[:240], rs_send.at[3]).wait()


def body(activations, output_grads, lengths, whitening):
    hbm = pl.BlockSpec(memory_space=pl.ANY)
    return pl.pallas_call(
        kernel,
        out_shape=jax.ShapeDtypeStruct((1, 128), F32),
        in_specs=[pl.BlockSpec(memory_space=pltpu.SMEM), hbm, hbm, hbm],
        out_specs=pl.BlockSpec(memory_space=pltpu.VMEM),
        scratch_shapes=[
            pltpu.VMEM((2, 32, 64, 128), BF),
            pltpu.VMEM((2, 32, 32, 128), BF),
            pltpu.VMEM((512, 2048), BF),
            pltpu.VMEM((512, 2048), BF),
            pltpu.VMEM((32, 2, 16, 128), BF),
            pltpu.VMEM((2, 2, 8, 2, 16, 128), BF),
            pltpu.VMEM((256, 2048), BF),
            pltpu.VMEM((256, 512), BF),
            pltpu.VMEM((256, 128), F32),
            pltpu.VMEM((15, 16, 128), F32),
            pltpu.VMEM((8, 16, 128), F32),
            pltpu.VMEM((4, 16, 128), F32),
            pltpu.VMEM((2, 16, 128), F32),
            pltpu.VMEM((256, 128), F32),
            pltpu.VMEM((128, 128), F32),
            pltpu.SemaphoreType.DMA((2, 8)),
            pltpu.SemaphoreType.DMA,
            pltpu.SemaphoreType.DMA,
            pltpu.SemaphoreType.DMA((2, 2)),
            pltpu.SemaphoreType.DMA((3, 4)),
            pltpu.SemaphoreType.DMA((3, 4)),
            pltpu.SemaphoreType.DMA((4,)),
            pltpu.SemaphoreType.DMA((4,)),
        ],
        compiler_params=pltpu.CompilerParams(
            collective_id=0, has_side_effects=True, vmem_limit_bytes=40 * 1024 * 1024
        ),
        cost_estimate=pl.CostEstimate(flops=700_000_000, bytes_accessed=4_000_000, transcendentals=0),
    )(lengths, activations, output_grads, whitening)


def solution(mesh):
    placed = (P("ex", "pp", None, None), P("ex", "pp", None, None), P("ex"), P("ex", "pp", None, None))

    def program(activations, output_grads, lengths, whitening):
        return jax.shard_map(body, mesh=mesh, in_specs=placed, out_specs=P("ex", None), check_vma=False)(
            activations, output_grads, lengths, whitening
        )

    return program
```

time: 119 us -> 62.1 us (0.52)
  blocking collectives: 89.5 us -> 0 us
  Pallas kernels: 0 us -> 56.8 us
  starting transfers between devices: 6.25 us -> 0 us
  matrix products: 5.98 us -> 0 us
  waiting for transfers between devices: 5.16 us -> 0 us
  other arithmetic: 4.16 us -> 0 us
  between operations: 2.27 us -> 0.01 us
    all_to_all x4 -> x0, blocking collectives: 89.5 us -> none  [the longest x1 48.7 us: body(): lax.all_to_all(sending, EX, split_axis=0, concat_axis=0, tiled=True)]
    pallas_call x0 -> x1, Pallas kernels: none -> 56.8 us  [body(): pl.pallas_call(kernel, out_shape=jax.ShapeDtypeStruct((1, 128), F32), in_...]
    all_to_all x1 -> x0, starting transfers between devices: 6.25 us -> none  [copy_for_each(): return lax.all_to_all(copies, axis, split_axis=0, concat_axis=0, tiled=True)]
    dot_general x6 -> x0, matrix products: 5.98 us -> none  [the longest x1 2.02 us: body(): jnp.einsum('emkt,emjt->mekj', masked, activations, preferred_element_type...]
    all_to_all x1 -> x0, waiting for transfers between devices: 5.16 us -> none  [copy_for_each(): return lax.all_to_all(copies, axis, split_axis=0, concat_axis=0, tiled=True)]
    unnamed x6 -> x9, local copies, waits for them, and re-layouts: 1.21 us -> 5.02 us
    all_to_all x2 -> x0, other arithmetic: 1.9 us -> none  [the longest x1 0.95 us: copy_for_each(): return lax.all_to_all(copies, axis, split_axis=0, concat_axis=0, tiled=True)]
    reshape x1 -> x0, local copies, waits for them, and re-layouts: 1.21 us -> none  [body(): lax.all_to_all(sending, EX, split_axis=0, concat_axis=0, tiled=True)]
  transfers between devices with their start and end apart: 1 -> 0, of which waited for: 1 -> 0; matrix products, arithmetic and copies ran while one was open for 0% -> 0% of each run, Pallas kernels for 0% -> 0%
where the time goes in v1:
time: 62.1 us; the launch traced here: 61.9 us
  Pallas kernels  56.8 us (91%)
  local copies, waits for them, and re-layouts  5.02 us (8%)
    pallas_call x1, Pallas kernels, body(): pl.pallas_call(kernel, out_shape=jax.ShapeDtypeStruct((1, 128), F32), in_...  56.8 us
    unnamed x9, local copies, waits for them, and re-layouts  5.02 us

profile of v1, /device:TPU:1, one launch (start us, length us, event | category | flops | bytes accessed | tf_op | source)
XLA Modules:
  0.0 61.9 jit_solution(7378324564618787115)
XLA Ops:
  0.0 0.0 copy-start
  0.0 1.6 %copy-done = bf16[1,1,512,2048]{3,2,1,0:T(8,128)(2,1)S(1)} copy-done((bf16[1,1,512,2048]{3,2,1,0:T(8,128)(2,1)S(1)}, bf16[1,1,512,2048]{3,2,1,0:T(8,128)(2,1)}, u32[]{:S(2)}) %copy-start) | copy-done | bytes 2097176
  1.6 0.0 copy-start.1
  1.6 1.2 %copy-done.1 = bf16[2,32,64,128]{3,2,1,0:T(8,128)(2,1)S(1)} copy-done((bf16[2,32,64,128]{3,2,1,0:T(8,128)(2,1)S(1)}, bf16[2,32,64,128]{3,2,1,0:T(8,128)(2,1)}, u32[]{:S(2)}) %copy-start.1) | copy-done | bytes 1048600
  2.8 0.0 copy-start.2
  2.8 1.0 %copy-done.2 = bf16[2,32,32,128]{3,2,1,0:T(8,128)(2,1)S(1)} copy-done((bf16[2,32,32,128]{3,2,1,0:T(8,128)(2,1)S(1)}, bf16[2,32,32,128]{3,2,1,0:T(8,128)(2,1)}, u32[]{:S(2)}) %copy-start.2) | copy-done | bytes 524312
  3.9 0.0 copy-start.3
  3.9 0.7 %copy-done.3 = s32[2]{0:T(128)S(1)} copy-done((s32[2]{0:T(128)S(1)}, s32[2]{0:T(128)}, u32[]{:S(2)}) %copy-start.3) | copy-done | bytes 32
  4.5 56.8 %shard_map.46 = f32[1,128]{1,0:T(1,128)S(1)} custom-call(s32[2]{0:T(128)S(1)} %copy-done.3, bf16[2,32,64,128]{3,2,1,0:T(8,128)(2,1)S(1)} %copy-done.1, bf16[2,32,32,128]{3,2,1,0:T(8,128)(2,1)S(1)} %copy-done.2, bf16[1,1,512,2048]{3,2,1,0:T(8,128)(2,1)S(1)} %copy-done), custom_call_target="tpu_custom_call" | custom-call | flops 700000000 | bytes 4000000 | tf_op jit(solution)/shard_map/pallas_call | solution.py:303
  61.3 0.5 copy.6
Async XLA Ops:
  0.0 1.6 %copy-start = (bf16[1,1,512,2048]{3,2,1,0:T(8,128)(2,1)S(1)}, bf16[1,1,512,2048]{3,2,1,0:T(8,128)(2,1)}, u32[]{:S(2)}) copy-start(bf16[1,1,512,2048]{3,2,1,0:T(8,128)(2,1)} %w_hbm.1) | copy-start | bytes 6291460
  1.6 1.2 %copy-start.1 = (bf16[2,32,64,128]{3,2,1,0:T(8,128)(2,1)S(1)}, bf16[2,32,64,128]{3,2,1,0:T(8,128)(2,1)}, u32[]{:S(2)}) copy-start(bf16[2,32,64,128]{3,2,1,0:T(8,128)(2,1)} %act_hbm.1) | copy-start | bytes 3145732
  2.8 1.0 %copy-start.2 = (bf16[2,32,32,128]{3,2,1,0:T(8,128)(2,1)S(1)}, bf16[2,32,32,128]{3,2,1,0:T(8,128)(2,1)}, u32[]{:S(2)}) copy-start(bf16[2,32,32,128]{3,2,1,0:T(8,128)(2,1)} %grad_hbm.1) | copy-start | bytes 1572868
  3.9 0.7 %copy-start.3 = (s32[2]{0:T(128)S(1)}, s32[2]{0:T(128)}, u32[]{:S(2)}) copy-start(s32[2]{0:T(128)} %len_ref.1) | copy-start | bytes 28

commit v2 on v1

--- a/solution.py
+++ b/solution.py
@@ -24,9 +24,9 @@
 
 
 def kernel(
-    len_ref, act_hbm, grad_hbm, w_hbm, out_ref,
-    act, grad, w_in, w, gbuf, near_buf, feat, white, part, rs_z, rs_y, rs_x, mine, full, answer,
-    in_sem, w_sem, p1_send, p1_recv, p2_send, p2_recv, rs_send, rs_recv,
+    len_hbm, act_hbm, grad_hbm, w_hbm, out_ref,
+    len_ref,     act, grad, w_in, w, gbuf, near_buf, shuffle, feat, white, part, rs_z, rs_y, rs_x, mine, full, answer,
+    len_sem, in_sem, w_sem, p1_send, p1_recv, p2_send, p2_recv, rs_send, rs_recv,
 ):
     ex = lax.axis_index("ex")
     x = lax.axis_index("pp")
@@ -40,103 +40,95 @@
     def at(y_, z_, c_, x_=None):
         return ((y_ * NZ + z_) * NC + c_, x if x_ is None else x_)
 
-    def row_of(i):
-        return (half + i // 4) % 2 * 4 + (y + i) % 4
-
-    def load(i):
-        rows = pl.ds(row_of(i) * 4, 4)
+    barrier = pltpu.get_barrier_semaphore()
+    toward = 2 * odd - 1
+
+    def greet(device):
+        pl.semaphore_signal(barrier, inc=1, device_id=device, device_id_type=MESH)
+
+    for dy in (4, 3, 5, 2, 6, 1, 7, 0):
+        for d in (3, 2, 1, 0):
+            if dy or d:
+                greet(at((y + dy) % NY, (z + toward * d + NZ) % NZ, c))
+    for i in (8, 9, 7, 6, 10, 11, 5, 4, 12, 13, 3, 2, 14, 15, 1):
+        j = (z * NC + c + i) % 16
+        greet(at(y, j // NC, j % NC))
+    for i in (2, 1, 3):
+        greet(at(y, z, c, (x + i) % NX))
+
+    len_copy = pltpu.make_async_copy(len_hbm, len_ref, len_sem)
+
+    def load(j):
+        rows = pl.ds(j * 8, 8)
         return (
-            pltpu.make_async_copy(act_hbm.at[:, rows], act.at[:, rows], in_sem.at[0, i]),
-            pltpu.make_async_copy(grad_hbm.at[:, rows], grad.at[:, rows], in_sem.at[1, i]),
+            pltpu.make_async_copy(act_hbm.at[:, rows], act.at[:, rows], in_sem.at[0, j]),
+            pltpu.make_async_copy(grad_hbm.at[:, rows], grad.at[:, rows], in_sem.at[1, j]),
         )
 
-    for i in range(NY):
-        for copy in load(i):
+    len_copy.start()
+    for j in range(4):
+        for copy in load(j):
             copy.start()
     w_copy = pltpu.make_async_copy(w_hbm.at[0, 0], w_in, w_sem)
     w_copy.start()
 
-    barrier = pltpu.get_barrier_semaphore()
-    toward = 2 * odd - 1
-
-    def greet(i, _):
-        y_, d = i // 4, i % 4
-
-        @pl.when(jnp.logical_not(jnp.logical_and(y_ == y, d == 0)))
-        def _():
-            z_ = (z + toward * d + NZ) % NZ
-            pl.semaphore_signal(barrier, inc=1, device_id=at(y_, z_, c), device_id_type=MESH)
-
-        return 0
-
-    lax.fori_loop(0, 32, greet, 0)
-    for i in range(1, 16):
-        j = (z * NC + c + i) % 16
-        pl.semaphore_signal(barrier, inc=1, device_id=at(y, j // NC, j % NC), device_id_type=MESH)
-    for i in range(1, NX):
-        pl.semaphore_signal(barrier, inc=1, device_id=at(y, z, c, (x + i) % NX), device_id_type=MESH)
-
     lane_low = lax.broadcasted_iota(jnp.int32, (16, 128), 1) < 64
     spots = lax.broadcasted_iota(jnp.int32, (1, 128), 1)
+    len_copy.wait()
     masks = [(spots < len_ref[e]).astype(F32).astype(BF) for e in range(2)]
 
-    s_own = ((z + 1) // 2) % 4
-    zl = (z + 1) % 2
-    slot = (y % 4) * 2 + zl
-
-    def target(p):
-        d = (2 * p - z + NZ) % NZ
-        chip = jnp.where(d < 4, 2 * p, 2 * p + 1)
-        far = jnp.where(d < 4, d // 2, (7 - d) // 2)
-        return chip, far
-
-    def gradients(i):
-        y_ = row_of(i)
-        for copy in load(i):
+    def gradients(j, _):
+        for copy in load(j):
             copy.wait()
-        for k in range(4):
-            m = y_ * 4 + k
+        for k in range(8):
+            m = j * 8 + k
             for e in range(2):
                 a = act[e, m]
                 g = grad[e, m] * masks[e]
                 twice = jnp.concatenate([a, a], axis=0)
                 both = lax.dot_general(g, twice, NT, preferred_element_type=F32)
                 gbuf[m, e] = jnp.where(lane_low, both[:16], both[16:]).astype(BF)
-
-    def send(i, _):
-        y_ = row_of(i)
-        for p in range(4):
-            m = y_ * 4 + p
-            chip, far = target(p)
-            here = jnp.logical_and(y_ == y, chip == z)
-
-            @pl.when(here)
-            def _():
-                pltpu.make_async_copy(
-                    gbuf.at[m], near_buf.at[half, far, slot], p1_recv.at[half, far]
-                ).start()
-
-            @pl.when(jnp.logical_not(here))
-            def _():
-                pltpu.make_async_remote_copy(
-                    src_ref=gbuf.at[m],
-                    dst_ref=near_buf.at[half, far, slot],
-                    send_sem=p1_send,
-                    recv_sem=p1_recv.at[half, far],
-                    device_id=at(y_, chip, c),
-                    device_id_type=MESH,
-                ).start()
-
-    gradients(0)
+        return 0
+
+    lax.fori_loop(0, 4, gradients, 0)
+
+    slot = (y % 4) * 2 + (z + 1) % 2
+
+    def send(group, _):
+        far = group % 2
+        for k in range(2):
+            p = (z // 2 + toward * (2 * far + k) + 4) % 4
+            chip = jnp.where((2 * p - z + NZ) % NZ < 4, 2 * p, 2 * p + 1)
+            for i in range(4):
+                y_ = (half + group // 2) % 2 * 4 + (y + i) % 4
+                m = y_ * 4 + p
+                here = jnp.logical_and(y_ == y, chip == z)
+
+                def remote():
+                    pltpu.make_async_remote_copy(
+                        src_ref=gbuf.at[m],
+                        dst_ref=near_buf.at[half, far, slot],
+                        send_sem=p1_send,
+                        recv_sem=p1_recv.at[half, far],
+                        device_id=at(y_, chip, c),
+                        device_id_type=MESH,
+                    ).start()
+
+                if k == 0 and i == 0:
+
+                    @pl.when(here)
+                    def _():
+                        pltpu.make_async_copy(
+                            gbuf.at[m], near_buf.at[half, far, slot], p1_recv.at[half, far]
+                        ).start()
+
+                    pl.when(jnp.logical_not(here))(remote)
+                else:
+                    remote()
+        return 0
+
     pl.semaphore_wait(barrier, 31 + 15 + 3)
-    send(0, 0)
-
-    def produce(i, _):
-        gradients(i)
-        send(i, 0)
-        return 0
-
-    lax.fori_loop(1, NY, produce, 0)
+    lax.fori_loop(0, 4, send, 0)
 
     w_copy.wait()
 
@@ -156,7 +148,7 @@
 
     to = lax.broadcasted_iota(jnp.int32, (256, 256), 0)
     frm = lax.broadcasted_iota(jnp.int32, (256, 256), 1)
-    shuffle = (frm == (to % 16) * 16 + to // 16).astype(F32).astype(BF)
+    shuffle[...] = (frm == (to % 16) * 16 + to // 16).astype(F32).astype(BF)
 
     def block_rows(q, z_, c_):
         h = (half + q // 2) % 2
@@ -188,7 +180,7 @@
         block = near_buf.at[h, q % 2]
         pltpu.make_async_copy(block, block, p1_recv.at[h, q % 2]).wait()
         tiles = near_buf[h, q % 2].reshape(256, 128)
-        turned = jnp.dot(shuffle, tiles, preferred_element_type=F32).astype(BF)
+        turned = jnp.dot(shuffle[...], tiles, preferred_element_type=F32).astype(BF)
         rows = block_rows(q, z, c)
         for kk in range(16):
             feat[rows, kk * 128:(kk + 1) * 128] = turned[kk * 16:(kk + 1) * 16]
@@ -208,7 +200,7 @@
         arrived(2, q)
     whiten((half + 1) % 2)
 
-    part[...] = lax.dot_general(white[...], white[128:], NT, preferred_element_type=F32)
+    part[...] = lax.dot_general(white[...], white[128:], NT, preferred_element_type=F32).astype(BF)
 
     me16 = z * NC + c
     for i in range(1, 16):
@@ -221,9 +213,9 @@
             device_id=at(y, j // NC, j % NC),
             device_id_type=MESH,
         ).start()
-    own = part[pl.ds(pl.multiple_of(me16 * 16, 16), 16)]
+    own = part[pl.ds(pl.multiple_of(me16 * 16, 16), 16)].astype(F32)
     pltpu.make_async_copy(rs_z, rs_z, rs_recv.at[0]).wait()
-    mine[0] = own + jnp.sum(rs_z[...], axis=0)
+    mine[0] = (own + jnp.sum(rs_z[...].astype(F32), axis=0)).astype(BF)
 
     for i in range(1, NY):
         pltpu.make_async_remote_copy(
@@ -236,7 +228,7 @@
         ).start()
     rs_y[y] = mine[0]
     pltpu.make_async_copy(rs_y.at[1:], rs_y.at[1:], rs_recv.at[1]).wait()
-    mine[1] = jnp.sum(rs_y[...], axis=0)
+    mine[1] = jnp.sum(rs_y[...].astype(F32), axis=0).astype(BF)
 
     for i in range(1, NX):
         pltpu.make_async_remote_copy(
@@ -250,7 +242,7 @@
     rs_x[x] = mine[1]
     pltpu.make_async_copy(rs_x.at[1:], rs_x.at[1:], rs_recv.at[2]).wait()
     my_rows = pl.ds(pl.multiple_of(me16 * 16, 16), 16)
-    full[my_rows] = jnp.sum(rs_x[...], axis=0)
+    full[my_rows] = jnp.sum(rs_x[...].astype(F32), axis=0).astype(BF)
 
     for i in range(1, 16):
         j = (me16 + i) % 16
@@ -265,18 +257,32 @@
     pltpu.make_async_copy(full.at[:240], full.at[:240], rs_recv.at[3]).wait()
 
     count = 32 * NX * 2048
-    scores = full[:128] * (1.0 / math.sqrt(count))
-    gram = full[128:] * (1.0 / count)
+    scores16 = full[:128] * BF(1.0 / math.sqrt(count))
+    gram = full[128:] * BF(1.0 / count)
+    scores = scores16.astype(F32)
     level = clip_frac * math.sqrt(128 * 128)
-    exact = functools.partial(jnp.dot, precision=lax.Precision.HIGHEST, preferred_element_type=F32)
+
+    def times_gram(value):
+        high = value.astype(BF)
+        rest = value - high.astype(F32)
+        middle = rest.astype(BF)
+        low = (rest - middle.astype(F32)).astype(BF)
+        product = jnp.dot(jnp.concatenate([high, middle, low], axis=0), gram, preferred_element_type=F32)
+        return product[:128] + product[128:256] + product[256:]
 
     def pace(residual):
         return jnp.minimum(step_rate, level * lax.rsqrt(total(residual * residual) + 1e-06))
 
-    now = pace(scores) * scores
-    for _ in range(2):
-        residual = scores - exact(now, gram) - ridge_shift * now
-        now = now + pace(residual) * residual
+    scores_gram = jnp.dot(scores16, gram, preferred_element_type=F32)
+    scores_gram2 = times_gram(scores_gram)
+    first = pace(scores)
+    now, now_gram = first * scores, first * scores_gram
+    residual = scores - now_gram - ridge_shift * now
+    residual_gram = scores_gram - first * scores_gram2 - ridge_shift * now_gram
+    second = pace(residual)
+    now, now_gram = now + second * residual, now_gram + second * residual_gram
+    residual = scores - now_gram - ridge_shift * now
+    now = now + pace(residual) * residual
     answer[...] = now
 
     q_y, q_z, q_c, q_e = ex // 32, (ex // 4) % 8, (ex // 2) % 2, ex % 2
@@ -286,7 +292,7 @@
     t_z = (t // 4) % 8
     spot = ((t_z + 1) // 2) % 4 * 32 + (t // 2) % 2 * 16 + t // 32 * 4 + (t_z + 1) % 2 * 2 + t % 2
     pick = (lax.broadcasted_iota(jnp.int32, (128, 128), 0) == spot).astype(F32)
-    out_ref[...] = exact(line, pick)[:1]
+    out_ref[...] = jnp.dot(line, pick, precision=lax.Precision.HIGHEST, preferred_element_type=F32)[:1]
 
     pltpu.make_async_copy(gbuf.at[:31], gbuf.at[:31], p1_send).wait()
     for kind in range(3):
@@ -299,29 +305,32 @@
 
 
 def body(activations, output_grads, lengths, whitening):
-    hbm = pl.BlockSpec(memory_space=pl.ANY)
+    hbm = pl.BlockSpec(memory_space=pltpu.HBM)
     return pl.pallas_call(
         kernel,
         out_shape=jax.ShapeDtypeStruct((1, 128), F32),
-        in_specs=[pl.BlockSpec(memory_space=pltpu.SMEM), hbm, hbm, hbm],
+        in_specs=[hbm, hbm, hbm, hbm],
         out_specs=pl.BlockSpec(memory_space=pltpu.VMEM),
         scratch_shapes=[
+            pltpu.SMEM((2,), jnp.int32),
             pltpu.VMEM((2, 32, 64, 128), BF),
             pltpu.VMEM((2, 32, 32, 128), BF),
             pltpu.VMEM((512, 2048), BF),
             pltpu.VMEM((512, 2048), BF),
             pltpu.VMEM((32, 2, 16, 128), BF),
             pltpu.VMEM((2, 2, 8, 2, 16, 128), BF),
+            pltpu.VMEM((256, 256), BF),
             pltpu.VMEM((256, 2048), BF),
             pltpu.VMEM((256, 512), BF),
-            pltpu.VMEM((256, 128), F32),
-            pltpu.VMEM((15, 16, 128), F32),
-            pltpu.VMEM((8, 16, 128), F32),
-            pltpu.VMEM((4, 16, 128), F32),
-            pltpu.VMEM((2, 16, 128), F32),
-            pltpu.VMEM((256, 128), F32),
+            pltpu.VMEM((256, 128), BF),
+            pltpu.VMEM((15, 16, 128), BF),
+            pltpu.VMEM((8, 16, 128), BF),
+            pltpu.VMEM((4, 16, 128), BF),
+            pltpu.VMEM((2, 16, 128), BF),
+            pltpu.VMEM((256, 128), BF),
             pltpu.VMEM((128, 128), F32),
-            pltpu.SemaphoreType.DMA((2, 8)),
+            pltpu.SemaphoreType.DMA,
+            pltpu.SemaphoreType.DMA((2, 4)),
             pltpu.SemaphoreType.DMA,
             pltpu.SemaphoreType.DMA,
             pltpu.SemaphoreType.DMA((2, 2)),
@@ -331,7 +340,7 @@
             pltpu.SemaphoreType.DMA((4,)),
         ],
         compiler_params=pltpu.CompilerParams(
-            collective_id=0, has_side_effects=True, vmem_limit_bytes=40 * 1024 * 1024
+            collective_id=0, has_side_effects=True, vmem_limit_bytes=62 * 1024 * 1024
         ),
         cost_estimate=pl.CostEstimate(flops=700_000_000, bytes_accessed=4_000_000, transcendentals=0),
     )(lengths, activations, output_grads, whitening)

time: 62.1 us -> 54.6 us (0.88)
  local copies, waits for them, and re-layouts: 5.02 us -> 1.19 us
  Pallas kernels: 56.8 us -> 53.3 us
    unnamed x9 -> x1, local copies, waits for them, and re-layouts: 5.02 us -> 1.19 us
    pallas_call x1, Pallas kernels: 56.8 us -> 53.3 us  [body(): pl.pallas_call(kernel, out_shape=jax.ShapeDtypeStruct((1, 128), F32), in_...]
where the time goes in v2:
time: 54.6 us; the launch traced here: 54.5 us
  Pallas kernels  53.3 us (98%)
  local copies, waits for them, and re-layouts  1.19 us (2%)
    pallas_call x1, Pallas kernels, body(): pl.pallas_call(kernel, out_shape=jax.ShapeDtypeStruct((1, 128), F32), in_...  53.3 us
    unnamed x1, local copies, waits for them, and re-layouts  1.19 us

profile of v2, /device:TPU:1, one launch (start us, length us, event | category | flops | bytes accessed | tf_op | source)
XLA Modules:
  0.0 54.5 jit_solution(10353884047115031181)
XLA Ops:
  0.0 53.3 %shard_map.46 = f32[1,128]{1,0:T(1,128)} custom-call(s32[2]{0:T(128)} %len_hbm.1, bf16[2,32,64,128]{3,2,1,0:T(8,128)(2,1)} %act_hbm.1, bf16[2,32,32,128]{3,2,1,0:T(8,128)(2,1)} %grad_hbm.1, bf16[1,1,512,2048]{3,2,1,0:T(8,128)(2,1)} %w_hbm.1), custom_call_target="tpu_custom_call" | custom-call | flops 700000000 | bytes 4000000 | tf_op jit(solution)/shard_map/pallas_call | solution.py:309
  53.3 1.2 %copy.6 = f32[1,128]{1,0:T(1,128)} copy(f32[1,128]{1,0:T(1,128)} %shard_map.46) | data formatting | bytes 1024

commit v3 on v2

v3 whole, which is shorter than its diff:
```python
import functools
import math

import jax
import jax.numpy as jnp
from jax import lax
from jax.experimental import pallas as pl
from jax.experimental.pallas import tpu as pltpu
from jax.sharding import PartitionSpec as P

MESH = pl.DeviceIdType.MESH
BF = jnp.bfloat16
F32 = jnp.float32
NY, NZ, NC, NX = 8, 8, 2, 4
NT = (((1,), (1,)), ((), ()))

step_rate = 0.5
ridge_shift = 0.5
clip_frac = 0.06


def total(value):
    return jnp.sum(jnp.sum(value, axis=1, keepdims=True), axis=0, keepdims=True)


def kernel(
    len_hbm, act_hbm, grad_hbm, w_hbm, out_ref,
    len_ref,     act, grad, w_in, w, gbuf, near_buf, shuffle, feat, white, part, rs_a, rs_z, rs_y, mine, full, answer,
    len_sem, in_sem, w_sem, p1_send, p1_recv, p2_send, p2_recv, rs_send, rs_recv,
):
    ex = lax.axis_index("ex")
    x = lax.axis_index("pp")
    y = ex // (NZ * NC)
    z = (ex // NC) % NZ
    c = ex % NC
    half = y // 4
    odd = z % 2
    mate_z = z + 1 - 2 * odd

    def at(y_, z_, c_, x_=None):
        return ((y_ * NZ + z_) * NC + c_, x if x_ is None else x_)

    barrier = pltpu.get_barrier_semaphore()
    toward = 2 * odd - 1

    def greet(device):
        pl.semaphore_signal(barrier, inc=1, device_id=device, device_id_type=MESH)

    for dy in (4, 3, 5, 2, 6, 1, 7, 0):
        for d in (3, 2, 1, 0):
            if dy or d:
                greet(at((y + dy) % NY, (z + toward * d + NZ) % NZ, c))
    for i in (4, 3, 5, 2, 6, 1, 7):
        greet(at(y, (z + i) % NZ, c))
    for i in (4, 5, 2, 3, 6, 7, 1):
        greet(at(y, z, (c + i) % 2, (x + i // 2) % NX))

    len_copy = pltpu.make_async_copy(len_hbm, len_ref, len_sem)

    def load(j):
        rows = pl.ds(j * 8, 8)
        return (
            pltpu.make_async_copy(act_hbm.at[:, rows], act.at[:, rows], in_sem.at[0, j]),
            pltpu.make_async_copy(grad_hbm.at[:, rows], grad.at[:, rows], in_sem.at[1, j]),
        )

    len_copy.start()
    for j in range(4):
        for copy in load(j):
            copy.start()
    w_copy = pltpu.make_async_copy(w_hbm.at[0, 0], w_in, w_sem)
    w_copy.start()

    lane_low = lax.broadcasted_iota(jnp.int32, (16, 128), 1) < 64
    spots = lax.broadcasted_iota(jnp.int32, (1, 128), 1)
    len_copy.wait()
    masks = [(spots < len_ref[e]).astype(F32).astype(BF) for e in range(2)]

    def gradients(j, _):
        for copy in load(j):
            copy.wait()
        for k in range(8):
            m = j * 8 + k
            for e in range(2):
                a = act[e, m]
                g = grad[e, m] * masks[e]
                twice = jnp.concatenate([a, a], axis=0)
                both = lax.dot_general(g, twice, NT, preferred_element_type=F32)
                gbuf[m, e] = jnp.where(lane_low, both[:16], both[16:]).astype(BF)
        return 0

    lax.fori_loop(0, 4, gradients, 0)

    slot = (y % 4) * 2 + (z + 1) % 2
    pl.semaphore_wait(barrier, 31 + 7 + 7)
    for far in range(2):
        for dy in (4, 3, 5, 2, 6, 1, 7, 0):
            y_ = (y + dy) % NY
            for k in range(2):
                p = (z // 2 + toward * (2 * far + k) + 4) % 4
                chip = jnp.where((2 * p - z + NZ) % NZ < 4, 2 * p, 2 * p + 1)
                source, target = gbuf.at[y_ * 4 + p], near_buf.at[half, far, slot]
                if dy == 0 and far == 0 and k == 0:
                    pltpu.make_async_copy(source, target, p1_recv.at[half, far]).start()
                else:
                    pltpu.make_async_remote_copy(
                        src_ref=source,
                        dst_ref=target,
                        send_sem=p1_send,
                        recv_sem=p1_recv.at[half, far],
                        device_id=at(y_, chip, c),
                        device_id_type=MESH,
                    ).start()

    w_copy.wait()

    def reorder(r, _):
        rows = pl.ds(r * 32, 32)
        low = lax.broadcasted_iota(jnp.int32, (32, 128), 1) < 64
        for a in range(8):
            t = w_in[rows, a * 128:(a + 1) * 128]
            u = w_in[rows, (8 + a) * 128:(9 + a) * 128]
            t_turned = jnp.concatenate([t[:, 64:], t[:, :64]], axis=1)
            u_turned = jnp.concatenate([u[:, 64:], u[:, :64]], axis=1)
            w[rows, 2 * a * 128:(2 * a + 1) * 128] = jnp.where(low, t, u_turned)
            w[rows, (2 * a + 1) * 128:(2 * a + 2) * 128] = jnp.where(low, t_turned, u)
        return 0

    lax.fori_loop(0, 16, reorder, 0)

    to = lax.broadcasted_iota(jnp.int32, (256, 256), 0)
    frm = lax.broadcasted_iota(jnp.int32, (256, 256), 1)
    shuffle[...] = (frm == (to % 16) * 16 + to // 16).astype(F32).astype(BF)

    def block_rows(q, z_, c_):
        h = 1 - q // 2
        p = z_ // 2
        s = jnp.where(z_ % 2 == 0, p - q % 2 + 4, p + 1 + q % 2) % 4
        return pl.ds(pl.multiple_of(h * 128 + s * 32 + c_ * 16, 16), 16)

    def pair_copy(kind, q):
        straight = kind == 2 and q == 3
        rows = block_rows(q, mate_z if kind == 2 and not straight else z, c)
        if straight:
            device = at(y, mate_z, 1 - c)
        else:
            device = at(y, mate_z, c) if kind == 0 else at(y, z, 1 - c)
        return pltpu.make_async_remote_copy(
            src_ref=feat.at[rows],
            dst_ref=feat.at[rows],
            send_sem=p2_send.at[kind, q],
            recv_sem=p2_recv.at[kind, q],
            device_id=device,
            device_id_type=MESH,
        )

    def arrived(kind, q):
        rows = block_rows(q, z if kind == 1 else mate_z, c if kind == 0 else 1 - c)
        pltpu.make_async_copy(feat.at[rows], feat.at[rows], p2_recv.at[kind, q]).wait()

    def whiten(h):
        white[h] = lax.dot_general(
            feat[h * 128:(h + 1) * 128], w[...], NT, preferred_element_type=F32
        ).astype(BF)

    me8 = x * NC + c

    def piece(j):
        return pl.ds(pl.multiple_of(j * 16, 16), 16)

    def copy_to(step, k, source, target, device):
        pltpu.make_async_remote_copy(
            src_ref=source,
            dst_ref=target,
            send_sem=rs_send.at[step, k],
            recv_sem=rs_recv.at[step, k],
            device_id=device,
            device_id_type=MESH,
        ).start()

    def await_seven(sems, step, k):
        pltpu.make_async_copy(rs_a.at[0], rs_a.at[0], sems.at[step, k]).wait()

    def scatter(k):
        part[k] = lax.dot_general(white[k], white[1], NT, preferred_element_type=F32)
        for i in (4, 5, 2, 3, 6, 7, 1):
            j = (me8 + i) % 8
            copy_to(0, k, part.at[k, piece(j)], rs_a.at[k, 7 - i], at(y, z, j % NC, j // NC))

    def over_z(k):
        await_seven(rs_recv, 0, k)
        mine[0, k] = part[k, piece(me8)] + jnp.sum(rs_a[k], axis=0)
        for i in (4, 3, 5, 2, 6, 1, 7):
            copy_to(1, k, mine.at[0, k], rs_z.at[k, z], at(y, (z + i) % NZ, c))
        rs_z[k, z] = mine[0, k]

    def over_y(k):
        await_seven(rs_recv, 1, k)
        mine[1, k] = jnp.sum(rs_z[k], axis=0)
        for i in (4, 3, 5, 2, 6, 1, 7):
            copy_to(2, k, mine.at[1, k], rs_y.at[k, y], at((y + i) % NY, z, c))
        rs_y[k, y] = mine[1, k]

    def gather(k):
        await_seven(rs_recv, 2, k)
        full[k, piece(me8)] = jnp.sum(rs_y[k], axis=0)
        for i in (4, 5, 2, 3, 6, 7, 1):
            j = (me8 + i) % 8
            copy_to(3, k, full.at[k, piece(me8)], full.at[k, piece(me8)], at(y, z, j % NC, j // NC))

    for q in range(4):
        h = 1 - q // 2
        block = near_buf.at[h, q % 2]
        pltpu.make_async_copy(block, block, p1_recv.at[h, q % 2]).wait()
        tiles = near_buf[h, q % 2].reshape(256, 128)
        turned = jnp.dot(shuffle[...], tiles, preferred_element_type=F32).astype(BF)
        rows = block_rows(q, z, c)
        for kk in range(16):
            feat[rows, kk * 128:(kk + 1) * 128] = turned[kk * 16:(kk + 1) * 16]
        pair_copy(0, q).start()
        if q == 3:
            pair_copy(2, q).start()
        pair_copy(1, q).start()
        if q > 0:
            arrived(0, q - 1)
            pair_copy(2, q - 1).start()
    for q in range(2):
        arrived(1, q)
        arrived(2, q)
    whiten(1)
    scatter(1)
    for q in range(2, 4):
        if q == 3:
            arrived(0, q)
        arrived(1, q)
        arrived(2, q)
    whiten(0)
    scatter(0)
    over_z(1)
    over_z(0)
    over_y(1)
    over_y(0)
    gather(1)
    gather(0)
    await_seven(rs_recv, 3, 1)
    await_seven(rs_recv, 3, 0)

    count = 32 * NX * 2048
    scores = full[0] * (1.0 / math.sqrt(count))
    gram = full[1] * (1.0 / count)
    level = clip_frac * math.sqrt(128 * 128)

    def times_gram(value):
        return jnp.dot(value, gram, precision=lax.Precision.HIGHEST, preferred_element_type=F32)

    def pace(residual):
        return jnp.minimum(step_rate, level * lax.rsqrt(total(residual * residual) + 1e-06))

    scores_gram = times_gram(scores)
    scores_gram2 = times_gram(scores_gram)
    first = pace(scores)
    now, now_gram = first * scores, first * scores_gram
    residual = scores - now_gram - ridge_shift * now
    residual_gram = scores_gram - first * scores_gram2 - ridge_shift * now_gram
    second = pace(residual)
    now, now_gram = now + second * residual, now_gram + second * residual_gram
    residual = scores - now_gram - ridge_shift * now
    now = now + pace(residual) * residual
    answer[...] = now

    q_y, q_z, q_c, q_e = ex // 32, (ex // 4) % 8, (ex // 2) % 2, ex % 2
    row = ((q_z + 1) // 2) % 4 * 32 + q_c * 16 + q_y * 4 + (q_z + 1) % 2 * 2 + q_e
    line = jnp.broadcast_to(answer[pl.ds(row, 1)], (8, 128))
    t = lax.broadcasted_iota(jnp.int32, (128, 128), 1)
    t_z = (t // 4) % 8
    spot = ((t_z + 1) // 2) % 4 * 32 + (t // 2) % 2 * 16 + t // 32 * 4 + (t_z + 1) % 2 * 2 + t % 2
    pick = (lax.broadcasted_iota(jnp.int32, (128, 128), 0) == spot).astype(F32)
    out_ref[...] = jnp.dot(line, pick, precision=lax.Precision.HIGHEST, preferred_element_type=F32)[:1]

    pltpu.make_async_copy(gbuf.at[:31], gbuf.at[:31], p1_send).wait()
    for kind in range(3):
        for q in range(4):
            pair_copy(kind, q).wait_send()
    for step in range(4):
        for k in range(2):
            await_seven(rs_send, step, k)


def body(activations, output_grads, lengths, whitening):
    hbm = pl.BlockSpec(memory_space=pltpu.HBM)
    return pl.pallas_call(
        kernel,
        out_shape=jax.ShapeDtypeStruct((1, 128), F32),
        in_specs=[hbm, hbm, hbm, hbm],
        out_specs=pl.BlockSpec(memory_space=pltpu.VMEM),
        scratch_shapes=[
            pltpu.SMEM((2,), jnp.int32),
            pltpu.VMEM((2, 32, 64, 128), BF),
            pltpu.VMEM((2, 32, 32, 128), BF),
            pltpu.VMEM((512, 2048), BF),
            pltpu.VMEM((512, 2048), BF),
            pltpu.VMEM((32, 2, 16, 128), BF),
            pltpu.VMEM((2, 2, 8, 2, 16, 128), BF),
            pltpu.VMEM((256, 256), BF),
            pltpu.VMEM((256, 2048), BF),
            pltpu.VMEM((2, 128, 512), BF),
            pltpu.VMEM((2, 128, 128), F32),
            pltpu.VMEM((2, 7, 16, 128), F32),
            pltpu.VMEM((2, 8, 16, 128), F32),
            pltpu.VMEM((2, 8, 16, 128), F32),
            pltpu.VMEM((2, 2, 16, 128), F32),
            pltpu.VMEM((2, 128, 128), F32),
            pltpu.VMEM((128, 128), F32),
            pltpu.SemaphoreType.DMA,
            pltpu.SemaphoreType.DMA((2, 4)),
            pltpu.SemaphoreType.DMA,
            pltpu.SemaphoreType.DMA,
            pltpu.SemaphoreType.DMA((2, 2)),
            pltpu.SemaphoreType.DMA((3, 4)),
            pltpu.SemaphoreType.DMA((3, 4)),
            pltpu.SemaphoreType.DMA((4, 2)),
            pltpu.SemaphoreType.DMA((4, 2)),
        ],
        compiler_params=pltpu.CompilerParams(
            collective_id=0, has_side_effects=True, vmem_limit_bytes=62 * 1024 * 1024
        ),
        cost_estimate=pl.CostEstimate(flops=700_000_000, bytes_accessed=4_000_000, transcendentals=0),
    )(lengths, activations, output_grads, whitening)


def solution(mesh):
    placed = (P("ex", "pp", None, None), P("ex", "pp", None, None), P("ex"), P("ex", "pp", None, None))

    def program(activations, output_grads, lengths, whitening):
        return jax.shard_map(body, mesh=mesh, in_specs=placed, out_specs=P("ex", None), check_vma=False)(
            activations, output_grads, lengths, whitening
        )

    return program
```

time: 54.6 us -> 53.3 us (0.976)
  Pallas kernels: 53.3 us -> 52 us
    pallas_call x1, Pallas kernels: 53.3 us -> 52 us  [body(): pl.pallas_call(kernel, out_shape=jax.ShapeDtypeStruct((1, 128), F32), in_...]
where the time goes in v3:
time: 53.3 us; the launch traced here: 53.2 us
  Pallas kernels  52 us (98%)
  local copies, waits for them, and re-layouts  1.19 us (2%)
    pallas_call x1, Pallas kernels, body(): pl.pallas_call(kernel, out_shape=jax.ShapeDtypeStruct((1, 128), F32), in_...  52 us
    unnamed x1, local copies, waits for them, and re-layouts  1.19 us

profile of v3, /device:TPU:1, one launch (start us, length us, event | category | flops | bytes accessed | tf_op | source)
XLA Modules:
  0.0 53.2 jit_solution(11552345105349256182)
XLA Ops:
  0.0 52.0 %shard_map.46 = f32[1,128]{1,0:T(1,128)} custom-call(s32[2]{0:T(128)} %len_hbm.1, bf16[2,32,64,128]{3,2,1,0:T(8,128)(2,1)} %act_hbm.1, bf16[2,32,32,128]{3,2,1,0:T(8,128)(2,1)} %grad_hbm.1, bf16[1,1,512,2048]{3,2,1,0:T(8,128)(2,1)} %w_hbm.1), custom_call_target="tpu_custom_call" | custom-call | flops 700000000 | bytes 4000000 | tf_op jit(solution)/shard_map/pallas_call | solution.py:291
  52.0 1.2 %copy.6 = f32[1,128]{1,0:T(1,128)} copy(f32[1,128]{1,0:T(1,128)} %shard_map.46) | data formatting | bytes 1024

commit v4 on v3

--- a/solution.py
+++ b/solution.py
@@ -54,6 +54,7 @@
         greet(at(y, (z + i) % NZ, c))
     for i in (4, 5, 2, 3, 6, 7, 1):
         greet(at(y, z, (c + i) % 2, (x + i // 2) % NX))
+    greet(at(y, mate_z, 1 - c))
 
     len_copy = pltpu.make_async_copy(len_hbm, len_ref, len_sem)
 
@@ -92,7 +93,7 @@
     lax.fori_loop(0, 4, gradients, 0)
 
     slot = (y % 4) * 2 + (z + 1) % 2
-    pl.semaphore_wait(barrier, 31 + 7 + 7)
+    pl.semaphore_wait(barrier, 31 + 7 + 7 + 1)
     for far in range(2):
         for dy in (4, 3, 5, 2, 6, 1, 7, 0):
             y_ = (y + dy) % NY
@@ -133,9 +134,9 @@
     shuffle[...] = (frm == (to % 16) * 16 + to // 16).astype(F32).astype(BF)
 
     def block_rows(q, z_, c_):
-        h = 1 - q // 2
+        h = 1 - q % 2
         p = z_ // 2
-        s = jnp.where(z_ % 2 == 0, p - q % 2 + 4, p + 1 + q % 2) % 4
+        s = jnp.where(z_ % 2 == 0, p - q // 2 + 4, p + 1 + q // 2) % 4
         return pl.ds(pl.multiple_of(h * 128 + s * 32 + c_ * 16, 16), 16)
 
     def pair_copy(kind, q):
@@ -209,10 +210,10 @@
             copy_to(3, k, full.at[k, piece(me8)], full.at[k, piece(me8)], at(y, z, j % NC, j // NC))
 
     for q in range(4):
-        h = 1 - q // 2
-        block = near_buf.at[h, q % 2]
-        pltpu.make_async_copy(block, block, p1_recv.at[h, q % 2]).wait()
-        tiles = near_buf[h, q % 2].reshape(256, 128)
+        h, far = 1 - q % 2, q // 2
+        block = near_buf.at[h, far]
+        pltpu.make_async_copy(block, block, p1_recv.at[h, far]).wait()
+        tiles = near_buf[h, far].reshape(256, 128)
         turned = jnp.dot(shuffle[...], tiles, preferred_element_type=F32).astype(BF)
         rows = block_rows(q, z, c)
         for kk in range(16):
@@ -221,15 +222,15 @@
         if q == 3:
             pair_copy(2, q).start()
         pair_copy(1, q).start()
-        if q > 0:
-            arrived(0, q - 1)
-            pair_copy(2, q - 1).start()
-    for q in range(2):
+    for q in range(3):
+        arrived(0, q)
+        pair_copy(2, q).start()
+    for q in (0, 2):
         arrived(1, q)
         arrived(2, q)
     whiten(1)
     scatter(1)
-    for q in range(2, 4):
+    for q in (1, 3):
         if q == 3:
             arrived(0, q)
         arrived(1, q)

time: 53.3 us -> 51.4 us (0.964)
  Pallas kernels: 52 us -> 50.1 us
    pallas_call x1, Pallas kernels: 52 us -> 50.1 us  [body(): pl.pallas_call(kernel, out_shape=jax.ShapeDtypeStruct((1, 128), F32), in_...]
where the time goes in v4:
time: 51.4 us; the launch traced here: 51.3 us
  Pallas kernels  50.1 us (97%)
  local copies, waits for them, and re-layouts  1.19 us (2%)
    pallas_call x1, Pallas kernels, body(): pl.pallas_call(kernel, out_shape=jax.ShapeDtypeStruct((1, 128), F32), in_...  50.1 us
    unnamed x1, local copies, waits for them, and re-layouts  1.19 us

profile of v4, /device:TPU:1, one launch (start us, length us, event | category | flops | bytes accessed | tf_op | source)
XLA Modules:
  0.0 51.3 jit_solution(13690912375866049352)
XLA Ops:
  0.0 50.1 %shard_map.46 = f32[1,128]{1,0:T(1,128)} custom-call(s32[2]{0:T(128)} %len_hbm.1, bf16[2,32,64,128]{3,2,1,0:T(8,128)(2,1)} %act_hbm.1, bf16[2,32,32,128]{3,2,1,0:T(8,128)(2,1)} %grad_hbm.1, bf16[1,1,512,2048]{3,2,1,0:T(8,128)(2,1)} %w_hbm.1), custom_call_target="tpu_custom_call" | custom-call | flops 700000000 | bytes 4000000 | tf_op jit(solution)/shard_map/pallas_call | solution.py:292
  50.1 1.2 %copy.6 = f32[1,128]{1,0:T(1,128)} copy(f32[1,128]{1,0:T(1,128)} %shard_map.46) | data formatting | bytes 1024

commit v5 on v4

--- a/solution.py
+++ b/solution.py
@@ -46,10 +46,11 @@
     def greet(device):
         pl.semaphore_signal(barrier, inc=1, device_id=device, device_id_type=MESH)
 
-    for dy in (4, 3, 5, 2, 6, 1, 7, 0):
-        for d in (3, 2, 1, 0):
-            if dy or d:
-                greet(at((y + dy) % NY, (z + toward * d + NZ) % NZ, c))
+    far_first = sorted(
+        [(dy, d) for dy in range(NY) for d in range(4) if dy or d], key=lambda v: -min(v[0], NY - v[0]) - v[1]
+    )
+    for dy, d in far_first:
+        greet(at((y + dy) % NY, (z + toward * d + NZ) % NZ, c))
     for i in (4, 3, 5, 2, 6, 1, 7):
         greet(at(y, (z + i) % NZ, c))
     for i in (4, 5, 2, 3, 6, 7, 1):
@@ -180,34 +181,38 @@
         ).start()
 
     def await_seven(sems, step, k):
-        pltpu.make_async_copy(rs_a.at[0], rs_a.at[0], sems.at[step, k]).wait()
+        pltpu.make_async_copy(rs_a[k], rs_a[k], sems.at[step, k]).wait()
+
+    def sum_of(stack):
+        return jnp.sum(stack[...].astype(F32), axis=0)
 
     def scatter(k):
-        part[k] = lax.dot_general(white[k], white[1], NT, preferred_element_type=F32)
+        part[k][...] = lax.dot_general(white[k], white[1], NT, preferred_element_type=F32).astype(part[k].dtype)
         for i in (4, 5, 2, 3, 6, 7, 1):
             j = (me8 + i) % 8
-            copy_to(0, k, part.at[k, piece(j)], rs_a.at[k, 7 - i], at(y, z, j % NC, j // NC))
+            copy_to(0, k, part[k].at[piece(j)], rs_a[k].at[7 - i], at(y, z, j % NC, j // NC))
 
     def over_z(k):
         await_seven(rs_recv, 0, k)
-        mine[0, k] = part[k, piece(me8)] + jnp.sum(rs_a[k], axis=0)
+        mine[k][0] = (part[k][piece(me8)].astype(F32) + sum_of(rs_a[k])).astype(part[k].dtype)
         for i in (4, 3, 5, 2, 6, 1, 7):
-            copy_to(1, k, mine.at[0, k], rs_z.at[k, z], at(y, (z + i) % NZ, c))
-        rs_z[k, z] = mine[0, k]
+            copy_to(1, k, mine[k].at[0], rs_z[k].at[z], at(y, (z + i) % NZ, c))
+        rs_z[k][z] = mine[k][0]
 
     def over_y(k):
         await_seven(rs_recv, 1, k)
-        mine[1, k] = jnp.sum(rs_z[k], axis=0)
+        mine[k][1] = sum_of(rs_z[k]).astype(part[k].dtype)
         for i in (4, 3, 5, 2, 6, 1, 7):
-            copy_to(2, k, mine.at[1, k], rs_y.at[k, y], at((y + i) % NY, z, c))
-        rs_y[k, y] = mine[1, k]
+            copy_to(2, k, mine[k].at[1], rs_y[k].at[y], at((y + i) % NY, z, c))
+        rs_y[k][y] = mine[k][1]
 
     def gather(k):
         await_seven(rs_recv, 2, k)
-        full[k, piece(me8)] = jnp.sum(rs_y[k], axis=0)
+        own = full[k].at[piece(me8)]
+        own[...] = sum_of(rs_y[k]).astype(part[k].dtype)
         for i in (4, 5, 2, 3, 6, 7, 1):
             j = (me8 + i) % 8
-            copy_to(3, k, full.at[k, piece(me8)], full.at[k, piece(me8)], at(y, z, j % NC, j // NC))
+            copy_to(3, k, own, own, at(y, z, j % NC, j // NC))
 
     for q in range(4):
         h, far = 1 - q % 2, q // 2
@@ -247,12 +252,17 @@
     await_seven(rs_recv, 3, 0)
 
     count = 32 * NX * 2048
-    scores = full[0] * (1.0 / math.sqrt(count))
-    gram = full[1] * (1.0 / count)
+    scores = full[0][...] * (1.0 / math.sqrt(count))
+    gram = full[1][...] * BF(1.0 / count)
     level = clip_frac * math.sqrt(128 * 128)
 
     def times_gram(value):
-        return jnp.dot(value, gram, precision=lax.Precision.HIGHEST, preferred_element_type=F32)
+        high = value.astype(BF)
+        rest = value - high.astype(F32)
+        middle = rest.astype(BF)
+        low = (rest - middle.astype(F32)).astype(BF)
+        product = jnp.dot(jnp.concatenate([high, middle, low], axis=0), gram, preferred_element_type=F32)
+        return product[:128] + product[128:256] + product[256:]
 
     def pace(residual):
         return jnp.minimum(step_rate, level * lax.rsqrt(total(residual * residual) + 1e-06))
@@ -266,17 +276,22 @@
     second = pace(residual)
     now, now_gram = now + second * residual, now_gram + second * residual_gram
     residual = scores - now_gram - ridge_shift * now
-    now = now + pace(residual) * residual
-    answer[...] = now
+    answer[0], answer[1] = now, residual
 
     q_y, q_z, q_c, q_e = ex // 32, (ex // 4) % 8, (ex // 2) % 2, ex % 2
     row = ((q_z + 1) // 2) % 4 * 32 + q_c * 16 + q_y * 4 + (q_z + 1) % 2 * 2 + q_e
-    line = jnp.broadcast_to(answer[pl.ds(row, 1)], (8, 128))
+    top = lax.broadcasted_iota(jnp.int32, (8, 128), 0) == 0
+    lines = jnp.where(
+        top,
+        jnp.broadcast_to(answer[0, pl.ds(row, 1)], (8, 128)),
+        jnp.broadcast_to(answer[1, pl.ds(row, 1)], (8, 128)),
+    )
     t = lax.broadcasted_iota(jnp.int32, (128, 128), 1)
     t_z = (t // 4) % 8
     spot = ((t_z + 1) // 2) % 4 * 32 + (t // 2) % 2 * 16 + t // 32 * 4 + (t_z + 1) % 2 * 2 + t % 2
     pick = (lax.broadcasted_iota(jnp.int32, (128, 128), 0) == spot).astype(F32)
-    out_ref[...] = jnp.dot(line, pick, precision=lax.Precision.HIGHEST, preferred_element_type=F32)[:1]
+    ordered = jnp.dot(lines, pick, precision=lax.Precision.HIGHEST, preferred_element_type=F32)
+    out_ref[...] = ordered[:1] + pace(residual) * ordered[1:2]
 
     pltpu.make_async_copy(gbuf.at[:31], gbuf.at[:31], p1_send).wait()
     for kind in range(3):
@@ -305,13 +320,13 @@
             pltpu.VMEM((256, 256), BF),
             pltpu.VMEM((256, 2048), BF),
             pltpu.VMEM((2, 128, 512), BF),
+            [pltpu.VMEM((128, 128), dtype) for dtype in (F32, BF)],
+            [pltpu.VMEM((7, 16, 128), dtype) for dtype in (F32, BF)],
+            [pltpu.VMEM((8, 16, 128), dtype) for dtype in (F32, BF)],
+            [pltpu.VMEM((8, 16, 128), dtype) for dtype in (F32, BF)],
+            [pltpu.VMEM((2, 16, 128), dtype) for dtype in (F32, BF)],
+            [pltpu.VMEM((128, 128), dtype) for dtype in (F32, BF)],
             pltpu.VMEM((2, 128, 128), F32),
-            pltpu.VMEM((2, 7, 16, 128), F32),
-            pltpu.VMEM((2, 8, 16, 128), F32),
-            pltpu.VMEM((2, 8, 16, 128), F32),
-            pltpu.VMEM((2, 2, 16, 128), F32),
-            pltpu.VMEM((2, 128, 128), F32),
-            pltpu.VMEM((128, 128), F32),
             pltpu.SemaphoreType.DMA,
             pltpu.SemaphoreType.DMA((2, 4)),
             pltpu.SemaphoreType.DMA,

time: 51.4 us -> 51.2 us (level)
  no operation moved by 1% of the time
where the time goes in v5:
time: 51.2 us; the launch traced here: 51 us
  Pallas kernels  49.8 us (97%)
  local copies, waits for them, and re-layouts  1.19 us (2%)
    pallas_call x1, Pallas kernels, body(): pl.pallas_call(kernel, out_shape=jax.ShapeDtypeStruct((1, 128), F32), in_...  49.8 us
    unnamed x1, local copies, waits for them, and re-layouts  1.19 us

profile of v5, /device:TPU:1, one launch (start us, length us, event | category | flops | bytes accessed | tf_op | source)
XLA Modules:
  0.0 51.0 jit_solution(9203263479110473347)
XLA Ops:
  0.0 49.8 %shard_map.46 = f32[1,128]{1,0:T(1,128)} custom-call(s32[2]{0:T(128)} %len_hbm.1, bf16[2,32,64,128]{3,2,1,0:T(8,128)(2,1)} %act_hbm.1, bf16[2,32,32,128]{3,2,1,0:T(8,128)(2,1)} %grad_hbm.1, bf16[1,1,512,2048]{3,2,1,0:T(8,128)(2,1)} %w_hbm.1), custom_call_target="tpu_custom_call" | custom-call | flops 700000000 | bytes 4000000 | tf_op jit(solution)/shard_map/pallas_call | solution.py:307
  49.8 1.2 %copy.6 = f32[1,128]{1,0:T(1,128)} copy(f32[1,128]{1,0:T(1,128)} %shard_map.46) | data formatting | bytes 1024

commit v6 on v5

--- a/solution.py
+++ b/solution.py
@@ -21,6 +21,14 @@
 
 def total(value):
     return jnp.sum(jnp.sum(value, axis=1, keepdims=True), axis=0, keepdims=True)
+
+
+def mod(value, size):
+    return lax.rem(value, jnp.int32(size))
+
+
+def div(value, size):
+    return lax.div(value, jnp.int32(size))
 
 
 def kernel(
@@ -30,11 +38,11 @@
 ):
     ex = lax.axis_index("ex")
     x = lax.axis_index("pp")
-    y = ex // (NZ * NC)
-    z = (ex // NC) % NZ
-    c = ex % NC
-    half = y // 4
-    odd = z % 2
+    y = div(ex, NZ * NC)
+    z = mod(div(ex, NC), NZ)
+    c = mod(ex, NC)
+    half = div(y, 4)
+    odd = mod(z, 2)
     mate_z = z + 1 - 2 * odd
 
     def at(y_, z_, c_, x_=None):
@@ -50,11 +58,11 @@
         [(dy, d) for dy in range(NY) for d in range(4) if dy or d], key=lambda v: -min(v[0], NY - v[0]) - v[1]
     )
     for dy, d in far_first:
-        greet(at((y + dy) % NY, (z + toward * d + NZ) % NZ, c))
+        greet(at(mod(y + dy, NY), mod(z + toward * d + NZ, NZ), c))
     for i in (4, 3, 5, 2, 6, 1, 7):
-        greet(at(y, (z + i) % NZ, c))
+        greet(at(y, mod(z + i, NZ), c))
     for i in (4, 5, 2, 3, 6, 7, 1):
-        greet(at(y, z, (c + i) % 2, (x + i // 2) % NX))
+        greet(at(y, z, mod(c + i, 2), mod(x + i // 2, NX)))
     greet(at(y, mate_z, 1 - c))
 
     len_copy = pltpu.make_async_copy(len_hbm, len_ref, len_sem)
@@ -97,10 +105,10 @@
     pl.semaphore_wait(barrier, 31 + 7 + 7 + 1)
     for far in range(2):
         for dy in (4, 3, 5, 2, 6, 1, 7, 0):
-            y_ = (y + dy) % NY
+            y_ = mod(y + dy, NY)
             for k in range(2):
-                p = (z // 2 + toward * (2 * far + k) + 4) % 4
-                chip = jnp.where((2 * p - z + NZ) % NZ < 4, 2 * p, 2 * p + 1)
+                p = mod(div(z, 2) + toward * (2 * far + k) + 4, 4)
+                chip = jnp.where(mod(2 * p - z + NZ, NZ) < 4, 2 * p, 2 * p + 1)
                 source, target = gbuf.at[y_ * 4 + p], near_buf.at[half, far, slot]
                 if dy == 0 and far == 0 and k == 0:
                     pltpu.make_async_copy(source, target, p1_recv.at[half, far]).start()
@@ -189,21 +197,21 @@
     def scatter(k):
         part[k][...] = lax.dot_general(white[k], white[1], NT, preferred_element_type=F32).astype(part[k].dtype)
         for i in (4, 5, 2, 3, 6, 7, 1):
-            j = (me8 + i) % 8
-            copy_to(0, k, part[k].at[piece(j)], rs_a[k].at[7 - i], at(y, z, j % NC, j // NC))
+            j = mod(me8 + i, 8)
+            copy_to(0, k, part[k].at[piece(j)], rs_a[k].at[7 - i], at(y, z, mod(j, NC), div(j, NC)))
 
     def over_z(k):
         await_seven(rs_recv, 0, k)
         mine[k][0] = (part[k][piece(me8)].astype(F32) + sum_of(rs_a[k])).astype(part[k].dtype)
         for i in (4, 3, 5, 2, 6, 1, 7):
-            copy_to(1, k, mine[k].at[0], rs_z[k].at[z], at(y, (z + i) % NZ, c))
+            copy_to(1, k, mine[k].at[0], rs_z[k].at[z], at(y, mod(z + i, NZ), c))
         rs_z[k][z] = mine[k][0]
 
     def over_y(k):
         await_seven(rs_recv, 1, k)
         mine[k][1] = sum_of(rs_z[k]).astype(part[k].dtype)
         for i in (4, 3, 5, 2, 6, 1, 7):
-            copy_to(2, k, mine[k].at[1], rs_y[k].at[y], at((y + i) % NY, z, c))
+            copy_to(2, k, mine[k].at[1], rs_y[k].at[y], at(mod(y + i, NY), z, c))
         rs_y[k][y] = mine[k][1]
 
     def gather(k):
@@ -211,8 +219,8 @@
         own = full[k].at[piece(me8)]
         own[...] = sum_of(rs_y[k]).astype(part[k].dtype)
         for i in (4, 5, 2, 3, 6, 7, 1):
-            j = (me8 + i) % 8
-            copy_to(3, k, own, own, at(y, z, j % NC, j // NC))
+            j = mod(me8 + i, 8)
+            copy_to(3, k, own, own, at(y, z, mod(j, NC), div(j, NC)))
 
     for q in range(4):
         h, far = 1 - q % 2, q // 2

time: 51.2 us -> 51.1 us (level)
  no operation moved by 1% of the time
where the time goes in v6:
time: 51.1 us; the launch traced here: 51 us
  Pallas kernels  49.8 us (97%)
  local copies, waits for them, and re-layouts  1.19 us (2%)
    pallas_call x1, Pallas kernels, body(): pl.pallas_call(kernel, out_shape=jax.ShapeDtypeStruct((1, 128), F32), in_...  49.8 us
    unnamed x1, local copies, waits for them, and re-layouts  1.19 us

profile of v6, /device:TPU:1, one launch (start us, length us, event | category | flops | bytes accessed | tf_op | source)
XLA Modules:
  0.0 51.0 jit_solution(16168463943983891575)
XLA Ops:
  0.0 49.8 %shard_map.46 = f32[1,128]{1,0:T(1,128)} custom-call(s32[2]{0:T(128)} %len_hbm.1, bf16[2,32,64,128]{3,2,1,0:T(8,128)(2,1)} %act_hbm.1, bf16[2,32,32,128]{3,2,1,0:T(8,128)(2,1)} %grad_hbm.1, bf16[1,1,512,2048]{3,2,1,0:T(8,128)(2,1)} %w_hbm.1), custom_call_target="tpu_custom_call" | custom-call | flops 700000000 | bytes 4000000 | tf_op jit(solution)/shard_map/pallas_call | solution.py:315
  49.8 1.2 %copy.6 = f32[1,128]{1,0:T(1,128)} copy(f32[1,128]{1,0:T(1,128)} %shard_map.46) | data formatting | bytes 1024
